TPU v7x, 32 devices: a whole 2x2x4 slice. The times are simulated.
32 devices in a mesh: grp: 2 (over x), ep: 16 (over z, y, core).
Axes of the slice: x: 2, y: 2, z: 4, core: 2. Of those that a mesh axis runs over, the one named last changes fastest.
Arguments:
- states: bfloat16 [2, 1280, 2048], P(None, ('grp', 'ep')), may hold values from -6 to 6
- route_ids: int32 [2, 1280, 8], P(None, ('grp', 'ep')), may hold values from 0 to 15, all different within a row; in each aligned block of 40 rows (0 to 39, 40 to 79, ..., all dimensions but the last counted through in order) at most 30 rows name the same one
- route_gates: float32 [2, 1280, 8], P(None, ('grp', 'ep')), may hold values from 0.02 to 0.3
- moe_gain: float32 [2048], replicated, may hold values from 0.25 to 1.75
- final_gain: float32 [2048], replicated, may hold values from 0.25 to 1.75
- gate_proj: bfloat16 [16, 2048, 512], P('ep', 'grp'), may hold values from -0.125 to 0.125
- up_proj: bfloat16 [16, 2048, 512], P('ep', 'grp'), may hold values from -0.125 to 0.125
- down_proj: bfloat16 [16, 512, 2048], P('ep', 'grp'), may hold values from -0.25 to 0.25
- old_slots: int32 [16], replicated, may hold values from 0 to 15, each once
- new_slots: int32 [16], replicated, may hold values from 0 to 15, each once
- req_lengths: int32 [2, 2, 4], P(None, 'grp'), may hold values from 1 to 320, 640 in all within a row
- head_proj: bfloat16 [2048, 49152], P(None, ('grp', 'ep')), may hold values from -14 to 14
Outputs:
- mixed: bfloat16 [2, 1280, 2048], P(None, ('grp', 'ep'))
- moved_gate: bfloat16 [16, 2048, 512], P('ep', 'grp')
- moved_up: bfloat16 [16, 2048, 512], P('ep', 'grp')
- moved_down: bfloat16 [16, 512, 2048], P('ep', 'grp')
- log_probs: float32 [2, 8, 49152], P(None, None, ('grp', 'ep'))
Inputs may be any that keep to these rules, and one draw needn't show every extreme that they name: `route_ids`: in each aligned block of 40 rows (the rows of one device in one batch) no expert is named by more than 30 rows, a bound that some block reaches; the 8 ids of a row differ. `old_slots`: each expert once. `new_slots`: each expert once. `req_lengths`: the 4 lengths of a group in a batch sum to 640, and the largest is 320.
All inputs are finite; a program needn't handle non-finite values.
Results may differ from a plain program's by a relative error of at most 0.0035.
Values may be sent and summed in bfloat16 or wider, within the bound.
A program may use at most 128 MiB of HBM per device.

v0:
```python
import jax
import jax.numpy as jnp
from jax import lax
from jax.sharding import PartitionSpec as P


def normalize(rows, gain):
    scale = lax.rsqrt(jnp.mean(rows * rows, axis=-1, keepdims=True) + 1e-06)
    return (rows * scale * gain).astype(jnp.bfloat16)


def owner_table(placement):
    ident = jnp.arange(placement.shape[0], dtype=jnp.int32)
    hits = placement[None, :] == ident[:, None]
    return jnp.sum(jnp.where(hits, ident[None, :], 0), axis=1)


def exchange(value, axis, bit):
    n = lax.axis_size(axis)
    return lax.ppermute(value, axis, [(i, i ^ bit) for i in range(n)])


def relocate(weights, source):
    n = source.shape[0]
    rows = weights.reshape(n, weights.shape[1] // n, weights.shape[2])
    spread = lax.all_to_all(rows, "ep", split_axis=0, concat_axis=0, tiled=True)
    ordered = jnp.take(spread, source, axis=0)
    moved = lax.all_to_all(ordered, "ep", split_axis=0, concat_axis=0, tiled=True)
    return moved.reshape(weights.shape)


def split_bf16(value):
    high = lax.reduce_precision(value, 8, 7)
    middle = lax.reduce_precision(value - high, 8, 7)
    low = value - high - middle
    return [part.astype(jnp.bfloat16) for part in (high, middle, low)]


def scatter_sum(terms):
    n = lax.axis_size("ep")
    me = lax.axis_index("ep")
    bit = 1
    held = terms
    while bit < n:
        pairs = held.reshape(held.shape[0] // 2, 2, *held.shape[1:])
        mine = me // bit % 2
        sent = lax.dynamic_index_in_dim(pairs, 1 - mine, 1, keepdims=False)
        kept = lax.dynamic_index_in_dim(pairs, mine, 1, keepdims=False)
        held = kept + exchange(sent.astype(jnp.bfloat16), "ep", bit).astype(jnp.float32)
        bit *= 2
    return held[0]


def butterfly(value, axis, join):
    bit = 1
    while bit < lax.axis_size(axis):
        value = join(value, exchange(value, axis, bit))
        bit *= 2
    return value


def join_stats(ours, theirs):
    top = jnp.maximum(ours[0], theirs[0])
    total = ours[1] * jnp.exp(ours[0] - top) + theirs[1] * jnp.exp(theirs[0] - top)
    return jnp.stack([top, total])


def per_device(
    states,
    route_ids,
    route_gates,
    moe_gain,
    final_gain,
    gate_proj,
    up_proj,
    down_proj,
    old_slots,
    new_slots,
    req_lengths,
    head_proj,
):
    n_ep = lax.axis_size("ep")
    n_grp = lax.axis_size("grp")
    column = lax.axis_index("ep")
    group = lax.axis_index("grp")
    batches, tok_rows, width = states.shape
    n_slots = old_slots.shape[0]
    old_owner = owner_table(old_slots)
    source = jnp.take(old_owner, new_slots)
    residual = states.astype(jnp.float32)
    normed = normalize(residual, moe_gain).reshape(-1, width)
    chosen = route_ids[..., None] == old_slots
    slot_gates = jnp.sum(jnp.where(chosen, route_gates[..., None], 0.0), axis=2)
    parts = split_bf16(slot_gates.reshape(-1, n_slots))
    extra = -(-len(parts) * n_slots // 128) * 128
    coded = jnp.pad(jnp.concatenate(parts, axis=1), ((0, 0), (0, extra - len(parts) * n_slots)))
    rows = lax.all_gather(jnp.concatenate([normed, coded], axis=1), "ep", axis=0, tiled=True)
    gate_full = lax.all_gather(gate_proj[0], "grp", axis=0, tiled=True)
    up_full = lax.all_gather(up_proj[0], "grp", axis=0, tiled=True)
    down_full = lax.all_gather(down_proj[0], "grp", axis=0, tiled=True)
    tokens = rows[:, :width]
    codes = rows[:, width : width + len(parts) * n_slots].astype(jnp.float32)
    codes = codes.reshape(-1, len(parts), n_slots)
    own = jnp.arange(n_slots, dtype=jnp.int32) == column
    weight = jnp.sum(jnp.where(own, codes, 0.0), axis=(1, 2))
    gate_vals = jnp.dot(tokens, gate_full, preferred_element_type=jnp.float32)
    up_vals = jnp.dot(tokens, up_full, preferred_element_type=jnp.float32)
    hidden = (jax.nn.silu(gate_vals) * up_vals).astype(jnp.bfloat16)
    outputs = jnp.dot(hidden, down_full, preferred_element_type=jnp.float32)
    terms = (outputs * weight[:, None]).reshape(n_ep, -1, width)
    summed = scatter_sum(terms).reshape(states.shape)
    mixed = (residual + summed).astype(jnp.bfloat16)
    moved = tuple((relocate(weights, source) for weights in (gate_proj, up_proj, down_proj)))
    request_ends = jnp.cumsum(req_lengths[:, 0, :], axis=-1) - 1
    local_ends = request_ends - column * tok_rows
    picker = (
        local_ends[:, :, None] == jnp.arange(tok_rows, dtype=jnp.int32)[None, None, :]
    ).astype(jnp.bfloat16)
    tails = jnp.einsum("brt,btd->brd", picker, mixed, preferred_element_type=jnp.float32).astype(
        jnp.bfloat16
    )
    add = lambda a, b: a + b
    tails = butterfly(tails, "ep", add)
    here = (jnp.arange(n_grp, dtype=jnp.int32) == group)[None, :, None, None]
    spread = jnp.where(here, tails[:, None], jnp.zeros((), jnp.bfloat16))
    spread = butterfly(spread, "grp", add)
    finals = normalize(spread.reshape(-1, width).astype(jnp.float32), final_gain)
    logits = jnp.dot(finals, head_proj, preferred_element_type=jnp.float32)
    top = jnp.max(logits, axis=1)
    total = jnp.sum(jnp.exp(logits - top[:, None]), axis=1)
    stats = jnp.stack([top, total])
    stats = butterfly(stats, "ep", join_stats)
    stats = butterfly(stats, "grp", join_stats)
    log_probs = (logits - stats[0][:, None] - jnp.log(stats[1])[:, None]).reshape(
        batches, -1, logits.shape[1]
    )
    return (mixed, *moved, log_probs)


def solution(mesh):
    placed = (
        P(None, ("grp", "ep"), None),
        P(None, ("grp", "ep"), None),
        P(None, ("grp", "ep"), None),
        P(),
        P(),
        P("ep", "grp", None),
        P("ep", "grp", None),
        P("ep", "grp", None),
        P(),
        P(),
        P(None, "grp", None),
        P(None, ("grp", "ep")),
    )
    return jax.shard_map(
        per_device,
        mesh=mesh,
        in_specs=placed,
        out_specs=(
            P(None, ("grp", "ep"), None),
            P("ep", "grp", None),
            P("ep", "grp", None),
            P("ep", "grp", None),
            P(None, None, ("grp", "ep")),
        ),
        check_vma=False,
    )
```

profile of v0, /device:TPU:0, one launch (start us, length us, event | category | flops | bytes accessed | tf_op | source)
XLA Modules:
  0.0 420.9 jit_solution(121535099977191811)
XLA Ops:
  8.2 1.1 fusion.20
  9.4 1.1 fusion.22
  13.5 58.4 %all-gather.8.cloned.1.call-done = bf16[1280,2176]{1,0:T(8,128)(2,1)} async-done(((bf16[80,2176]{1,0:T(8,128)(2,1)}), bf16[1280,2176]{1,0:T(8,128)(2,1)}) %all-gather.8.cloned.1.call-update) | async-done | bytes 5570576 | tf_op jit(solution)/shard_map/all_gather | solution.py:97
  71.9 1.2 select_reduce_fusion
  73.1 32.1 %all-gather.10.cloned.1.call-done = bf16[1,2048,512]{2,1,0:T(8,128)(2,1)} async-done(((bf16[1,1024,512]{2,1,0:T(8,128)(2,1)}), bf16[1,2048,512]{2,1,0:T(8,128)(2,1)}) %all-gather.10.cloned.1.call-update) | async-done | bytes 2097168 | tf_op jit(solution)/shard_map/all_gather | solution.py:98
  105.2 5.4 %fusion.2 = f32[1280,512]{1,0:T(8,128)S(1)} fusion(bf16[1280,2176]{1,0:T(8,128)(2,1)} %all-gather.8.cloned.1.call-done, bf16[1,2048,512]{2,1,0:T(8,128)(2,1)} %all-gather.10.cloned.1.call-done), kind=kOutput, calls=%fused_computation.9 | convolution fusion | flops 2684354560 | bytes 9961472 | tf_op jit(solution)/shard_map/dot_general | solution.py:106
  110.6 29.3 %all-gather.14.cloned.1.call-done = bf16[1,512,2048]{2,1,0:T(8,128)(2,1)} async-done(((bf16[1,256,2048]{2,1,0:T(8,128)(2,1)}), bf16[1,512,2048]{2,1,0:T(8,128)(2,1)}) %all-gather.14.cloned.1.call-update) | async-done | bytes 2097168 | tf_op jit(solution)/shard_map/all_gather | solution.py:100
  139.9 34.6 %all-gather.12.cloned.1.call-done = bf16[1,2048,512]{2,1,0:T(8,128)(2,1)} async-done(((bf16[1,1024,512]{2,1,0:T(8,128)(2,1)}), bf16[1,2048,512]{2,1,0:T(8,128)(2,1)}) %all-gather.12.cloned.1.call-update) | async-done | bytes 2097168 | tf_op jit(solution)/shard_map/all_gather | solution.py:99
  174.5 11.4 %convolution_multiply_fusion = f32[1280,2048]{1,0:T(8,128)} fusion(f32[1280]{0:T(1024)S(1)} %select_reduce_fusion, bf16[1,512,2048]{2,1,0:T(8,128)(2,1)} %all-gather.14.cloned.1.call-done, bf16[1280,2176]{1,0:T(8,128)(2,1)} %all-gather.8.cloned.1.call-done, f32[1280,512]{1,0:T(8,128)S(1)} %fusion.2, bf16[1,2048,512]{2,1,0:T(8,128)(2,1)} %all-gather.12.cloned.1.call-done), kind=kOutput, calls=%fused_computation.4 | convolution fusion | flops 5375262720 | bytes 22549504 | tf_op jit(solution)/shard_map/dot_general | solution.py:109
  185.9 4.5 %fusion.10 = bf16[8,80,2048]{2,1,0:T(8,128)(2,1)} fusion(f32[8,2,80,2048]{3,2,1,0:T(8,128)} %bitcast.149, s32[]{:T(128)S(6)} %select_n.112), kind=kLoop, calls=%fused_computation.13 | loop fusion | bytes 5242884 | tf_op jit(solution)/shard_map/convert_element_type | solution.py:49
  190.3 30.5 %all_to_all.30 = bf16[16,64,512]{2,1,0:T(8,128)(2,1)} all-to-all(bf16[16,64,512]{2,1,0:T(8,128)(2,1)S(1)} %bitcast.151), channel_id=1, replica_groups=mesh['grp'=2,'ep'=16] {'ep'}, dimensions={0} | all-to-all | bytes 2097152 | tf_op jit(solution)/shard_map/all_to_all | solution.py:26
  220.8 5.0 %all-to-all-start = ((bf16[16,64,512]{2,1,0:T(8,128)(2,1)}), bf16[16,64,512]{2,1,0:T(8,128)(2,1)S(1)}, u32[]{:S(2)}, u32[]{:S(2)}) async-start(bf16[16,64,512]{2,1,0:T(8,128)(2,1)} %bitcast.14), calls=%async_computation | async-start | bytes 2097152 | tf_op jit(solution)/shard_map/all_to_all | solution.py:26
  225.9 4.1 bitcast_add_fusion
  230.0 2.3 copy-done
  232.5 1.9 collective-permute-start.1
  234.5 14.4 %all-to-all-done = bf16[16,64,512]{2,1,0:T(8,128)(2,1)S(1)} async-done(((bf16[16,64,512]{2,1,0:T(8,128)(2,1)}), bf16[16,64,512]{2,1,0:T(8,128)(2,1)S(1)}, u32[]{:S(2)}, u32[]{:S(2)}) %all-to-all-start) | async-done | bytes 1048608 | tf_op jit(solution)/shard_map/all_to_all | solution.py:26
  248.8 7.0 %all-to-all-start.4 = ((bf16[16,16,2048]{2,1,0:T(8,128)(2,1)}), bf16[16,16,2048]{2,1,0:T(8,128)(2,1)}, u32[]{:S(2)}, u32[]{:S(2)}) async-start(bf16[16,16,2048]{2,1,0:T(8,128)(2,1)} %bitcast.18), calls=%async_computation.4 | async-start | bytes 2097152 | tf_op jit(solution)/shard_map/all_to_all | solution.py:26
  256.7 19.4 %collective-permute-done.1 = bf16[4,80,2048]{2,1,0:T(8,128)(2,1)} collective-permute-done((bf16[4,80,2048]{2,1,0:T(8,128)(2,1)S(1)}, bf16[4,80,2048]{2,1,0:T(8,128)(2,1)}, u32[]{:S(2)}, u32[]{:S(2)}) %collective-permute-start.1) | collective-permute-done | bytes 1310752 | tf_op jit(solution)/shard_map/ppermute | solution.py:20
  276.1 2.4 bitcast_add_fusion.1
  279.5 3.7 collective-permute-start.2
  283.1 2.8 gather_fusion.3
  286.0 2.8 gather_fusion.2
  288.8 3.1 broadcast_select_fusion
  291.9 5.1 %all-to-all-start.1 = ((bf16[16,64,512]{2,1,0:T(8,128)(2,1)}), bf16[16,64,512]{2,1,0:T(8,128)(2,1)}, u32[]{:S(2)}, u32[]{:S(2)}) async-start(bf16[16,64,512]{2,1,0:T(8,128)(2,1)} %get-tuple-element.22), calls=%async_computation.1 | async-start | bytes 2097152 | tf_op jit(solution)/shard_map/all_to_all | solution.py:28
  297.6 1.2 bitcast_add_fusion.2
  298.9 1.1 copy-done.3
  300.0 2.3 collective-permute-start.3
  302.4 35.1 %collective-permute-done.3 = bf16[1,80,2048]{2,1,0:T(8,128)(2,1)S(1)} collective-permute-done((bf16[1,80,2048]{2,1,0:T(8,128)(2,1)S(1)}, bf16[1,80,2048]{2,1,0:T(8,128)(2,1)S(1)}, u32[]{:S(2)}, u32[]{:S(2)}) %collective-permute-start.3) | collective-permute-done | bytes 327712 | tf_op jit(solution)/shard_map/ppermute | solution.py:20
  337.5 1.1 convert_add_fusion.1
  338.7 3.7 all-to-all-start.3
  344.1 1.9 collective-permute-start.5
  346.0 5.7 %collective-permute-done.5 = bf16[2,4,2048]{2,1,0:T(4,128)(2,1)S(1)} collective-permute-done((bf16[2,4,2048]{2,1,0:T(4,128)(2,1)S(1)}, bf16[2,4,2048]{2,1,0:T(4,128)(2,1)S(1)}, u32[]{:S(2)}, u32[]{:S(2)}) %collective-permute-start.5) | collective-permute-done | bytes 32800 | tf_op jit(solution)/shard_map/ppermute | solution.py:20
  351.8 9.5 %collective-permute-done.6 = bf16[2,4,2048]{2,1,0:T(4,128)(2,1)S(1)} collective-permute-done((bf16[2,4,2048]{2,1,0:T(4,128)(2,1)S(1)}, bf16[2,4,2048]{2,1,0:T(4,128)(2,1)S(1)}, u32[]{:S(2)}, u32[]{:S(2)}) %collective-permute-start.6) | collective-permute-done | bytes 32800 | tf_op jit(solution)/shard_map/ppermute | solution.py:20
  361.3 4.5 %collective-permute-start.7 = (bf16[2,4,2048]{2,1,0:T(4,128)(2,1)S(1)}, bf16[2,4,2048]{2,1,0:T(4,128)(2,1)S(1)}, u32[]{:S(2)}, u32[]{:S(2)}) collective-permute-start(bf16[2,4,2048]{2,1,0:T(4,128)(2,1)S(1)} %add.202), channel_id=1, source_target_pairs={{0,8},{1,9},{2,10},{3,11},{4,12},{5,13},{6,14},{7,15},{8,0},{9,1},... | collective-permute-start | bytes 98312 | tf_op jit(solution)/shard_map/ppermute | solution.py:20
  365.8 1.8 gather_fusion.1
  367.6 2.8 collective-permute-done.7
  371.2 1.1 broadcast_select_fusion.2
  372.3 2.6 collective-permute-done.8
  375.4 3.7 all-to-all-start.5
  379.1 3.9 fusion.47
  384.5 1.9 collective-permute-start.10
  386.4 1.7 collective-permute-done.10
  388.2 1.9 collective-permute-start.11
  390.1 7.2 %collective-permute-done.11 = f32[2,16]{1,0:T(2,128)S(1)} collective-permute-done((f32[2,16]{1,0:T(2,128)S(1)}, f32[2,16]{1,0:T(2,128)S(1)}, u32[]{:S(2)}, u32[]{:S(2)}) %collective-permute-start.11) | collective-permute-done | bytes 160 | tf_op jit(solution)/shard_map/ppermute | solution.py:20
  397.3 4.4 %collective-permute-start.12 = (f32[2,16]{1,0:T(2,128)S(1)}, f32[2,16]{1,0:T(2,128)S(1)}, u32[]{:S(2)}, u32[]{:S(2)}) collective-permute-start(f32[2,16]{1,0:T(2,128)S(1)} %pad_maximum_fusion.4), channel_id=1, source_target_pairs={{0,8},{1,9},{2,10},{3,11},{4,12},{5,13},{6,14},{7,15},{8,0},{9,1},... | collective-permute-start | bytes 392 | tf_op jit(solution)/shard_map/ppermute | solution.py:20
  401.7 4.0 collective-permute-done.12
  406.4 3.0 collective-permute-done.13
  410.1 2.3 copy.33
  (89 shorter events, 14.6 us)
Async XLA Ops:
  7.2 64.8 %all-gather.8.cloned.1.call-start = ((), (), s32[]{:S(2)}) async-start(), calls=%async_computation.6 | async-start | bytes 5918720 | tf_op jit(solution)/shard_map/all_gather | solution.py:97
  11.3 93.9 %all-gather.10.cloned.1.call-start = ((), (), s32[]{:S(2)}) async-start(), calls=%async_computation.7 | async-start | bytes 3145728 | tf_op jit(solution)/shard_map/all_gather | solution.py:98
  12.1 127.8 %all-gather.14.cloned.1.call-start = ((), (), s32[]{:S(2)}) async-start(), calls=%async_computation.9 | async-start | bytes 3145728 | tf_op jit(solution)/shard_map/all_gather | solution.py:100
  12.8 161.7 %all-gather.12.cloned.1.call-start = ((), (), s32[]{:S(2)}) async-start(), calls=%async_computation.8 | async-start | bytes 3145728 | tf_op jit(solution)/shard_map/all_gather | solution.py:99
  185.9 4.5 %copy-start.2 = (bf16[1,1024,512]{2,1,0:T(8,128)(2,1)S(1)}, bf16[1,1024,512]{2,1,0:T(8,128)(2,1)}, u32[]{:S(2)}) copy-start(bf16[1,1024,512]{2,1,0:T(8,128)(2,1)} %param.20) | copy-start | bytes 3145732
  190.3 35.5 %collective-permute-start = (bf16[8,80,2048]{2,1,0:T(8,128)(2,1)}, bf16[8,80,2048]{2,1,0:T(8,128)(2,1)}, u32[]{:S(2)}, u32[]{:S(2)}) collective-permute-start(bf16[8,80,2048]{2,1,0:T(8,128)(2,1)} %fusion.10), channel_id=1, source_target_pairs={{0,1},{1,0},{2,3},{3,2},{4,5},{5,4},{6,7},{7,6},{8,9},{9,8},{10,11... | collective-permute-start | bytes 7864328 | tf_op jit(solution)/shard_map/ppermute | solution.py:20
  220.8 28.0 %all-to-all-start = ((bf16[16,64,512]{2,1,0:T(8,128)(2,1)}), bf16[16,64,512]{2,1,0:T(8,128)(2,1)S(1)}, u32[]{:S(2)}, u32[]{:S(2)}) async-start(bf16[16,64,512]{2,1,0:T(8,128)(2,1)} %bitcast.14), calls=%async_computation | async-start | bytes 2097152 | tf_op jit(solution)/shard_map/all_to_all | solution.py:26
  230.0 2.3 copy-start
  230.0 25.9 %copy-start.9 = (s32[16]{0:T(128)S(1)}, s32[16]{0:T(128)}, u32[]{:S(2)}) copy-start(s32[16]{0:T(128)} %param.23) | copy-start | bytes 196
  230.0 25.9 %copy-start.8 = (s32[16]{0:T(128)S(1)}, s32[16]{0:T(128)}, u32[]{:S(2)}) copy-start(s32[16]{0:T(128)} %param.22) | copy-start | bytes 196
  232.5 43.6 %collective-permute-start.1 = (bf16[4,80,2048]{2,1,0:T(8,128)(2,1)S(1)}, bf16[4,80,2048]{2,1,0:T(8,128)(2,1)}, u32[]{:S(2)}, u32[]{:S(2)}) collective-permute-start(bf16[4,80,2048]{2,1,0:T(8,128)(2,1)S(1)} %fusion.14), channel_id=1, source_target_pairs={{0,2},{1,3},{2,0},{3,1},{4,6},{5,7},{6,4},{7,5},{8,10},{9,11},{10,... | collective-permute-start | bytes 3932168 | tf_op jit(solution)/shard_map/ppermute | solution.py:20
  248.8 7.1 %copy-start.1 = (bf16[16,64,512]{2,1,0:T(8,128)(2,1)}, bf16[16,64,512]{2,1,0:T(8,128)(2,1)S(1)}, u32[]{:S(2)}) copy-start(bf16[16,64,512]{2,1,0:T(8,128)(2,1)S(1)} %all-to-all-done) | copy-start | bytes 3145732
  248.8 43.1 %all-to-all-start.4 = ((bf16[16,16,2048]{2,1,0:T(8,128)(2,1)}), bf16[16,16,2048]{2,1,0:T(8,128)(2,1)}, u32[]{:S(2)}, u32[]{:S(2)}) async-start(bf16[16,16,2048]{2,1,0:T(8,128)(2,1)} %bitcast.18), calls=%async_computation.4 | async-start | bytes 2097152 | tf_op jit(solution)/shard_map/all_to_all | solution.py:26
  279.5 18.2 %collective-permute-start.2 = (bf16[2,80,2048]{2,1,0:T(8,128)(2,1)}, bf16[2,80,2048]{2,1,0:T(8,128)(2,1)}, u32[]{:S(2)}, u32[]{:S(2)}) collective-permute-start(bf16[2,80,2048]{2,1,0:T(8,128)(2,1)} %fusion.24), channel_id=1, source_target_pairs={{0,4},{1,5},{2,6},{3,7},{4,0},{5,1},{6,2},{7,3},{8,12},{9,13},{10,... | collective-permute-start | bytes 1966088 | tf_op jit(solution)/shard_map/ppermute | solution.py:20
  291.9 10.3 %copy-start.7 = (s32[2,1,4]{2,1,0:T(1,128)S(1)}, s32[2,1,4]{2,1,0:T(1,128)}, u32[]{:S(2)}) copy-start(s32[2,1,4]{2,1,0:T(1,128)} %param.24) | copy-start | bytes 100
  291.9 46.9 %all-to-all-start.1 = ((bf16[16,64,512]{2,1,0:T(8,128)(2,1)}), bf16[16,64,512]{2,1,0:T(8,128)(2,1)}, u32[]{:S(2)}, u32[]{:S(2)}) async-start(bf16[16,64,512]{2,1,0:T(8,128)(2,1)} %get-tuple-element.22), calls=%async_computation.1 | async-start | bytes 2097152 | tf_op jit(solution)/shard_map/all_to_all | solution.py:28
  297.0 41.7 %copy-start.4 = (bf16[2,40,2048]{2,1,0:T(8,128)(2,1)S(1)}, bf16[2,40,2048]{2,1,0:T(8,128)(2,1)}, u32[]{:S(2)}) copy-start(bf16[2,40,2048]{2,1,0:T(8,128)(2,1)} %param.14) | copy-start | bytes 983044
  298.8 1.1 copy-start.3
  300.0 37.5 %collective-permute-start.3 = (bf16[1,80,2048]{2,1,0:T(8,128)(2,1)S(1)}, bf16[1,80,2048]{2,1,0:T(8,128)(2,1)S(1)}, u32[]{:S(2)}, u32[]{:S(2)}) collective-permute-start(bf16[1,80,2048]{2,1,0:T(8,128)(2,1)S(1)} %dynamic-slice_convert_fusion.2), channel_id=1, source_target_pairs={{0,8},{1,9},{2,10},{3,11},{4,12},{5,13},{6,14},{7,15},{8,0},{9,1},... | collective-permute-start | bytes 983048 | tf_op jit(solution)/shard_map/ppermute | solution.py:20
  338.7 33.6 %copy-start.5 = (bf16[2,40,2048]{2,1,0:T(8,128)(2,1)}, bf16[2,40,2048]{2,1,0:T(8,128)(2,1)S(1)}, u32[]{:S(2)}) copy-start(bf16[2,40,2048]{2,1,0:T(8,128)(2,1)S(1)} %fusion.23) | copy-start | bytes 983044
  338.7 36.6 %all-to-all-start.3 = ((bf16[16,64,512]{2,1,0:T(8,128)(2,1)}), bf16[16,64,512]{2,1,0:T(8,128)(2,1)S(1)}, u32[]{:S(2)}, u32[]{:S(2)}) async-start(bf16[16,64,512]{2,1,0:T(8,128)(2,1)} %get-tuple-element.21), calls=%async_computation.3 | async-start | bytes 2097152 | tf_op jit(solution)/shard_map/all_to_all | solution.py:28
  342.7 1.3 collective-permute-start.4
  344.1 7.6 %collective-permute-start.5 = (bf16[2,4,2048]{2,1,0:T(4,128)(2,1)S(1)}, bf16[2,4,2048]{2,1,0:T(4,128)(2,1)S(1)}, u32[]{:S(2)}, u32[]{:S(2)}) collective-permute-start(bf16[2,4,2048]{2,1,0:T(4,128)(2,1)S(1)} %add.200), channel_id=1, source_target_pairs={{0,2},{1,3},{2,0},{3,1},{4,6},{5,7},{6,4},{7,5},{8,10},{9,11},{10,... | collective-permute-start | bytes 98312 | tf_op jit(solution)/shard_map/ppermute | solution.py:20
  351.8 9.5 %collective-permute-start.6 = (bf16[2,4,2048]{2,1,0:T(4,128)(2,1)S(1)}, bf16[2,4,2048]{2,1,0:T(4,128)(2,1)S(1)}, u32[]{:S(2)}, u32[]{:S(2)}) collective-permute-start(bf16[2,4,2048]{2,1,0:T(4,128)(2,1)S(1)} %add.201), channel_id=1, source_target_pairs={{0,4},{1,5},{2,6},{3,7},{4,0},{5,1},{6,2},{7,3},{8,12},{9,13},{10,... | collective-permute-start | bytes 98312 | tf_op jit(solution)/shard_map/ppermute | solution.py:20
  361.3 9.1 %collective-permute-start.7 = (bf16[2,4,2048]{2,1,0:T(4,128)(2,1)S(1)}, bf16[2,4,2048]{2,1,0:T(4,128)(2,1)S(1)}, u32[]{:S(2)}, u32[]{:S(2)}) collective-permute-start(bf16[2,4,2048]{2,1,0:T(4,128)(2,1)S(1)} %add.202), channel_id=1, source_target_pairs={{0,8},{1,9},{2,10},{3,11},{4,12},{5,13},{6,14},{7,15},{8,0},{9,1},... | collective-permute-start | bytes 98312 | tf_op jit(solution)/shard_map/ppermute | solution.py:20
  367.6 11.5 %copy-start.6 = (f32[2048]{0:T(1024)S(1)}, f32[2048]{0:T(1024)}, u32[]{:S(2)}) copy-start(f32[2048]{0:T(1024)} %param.18) | copy-start | bytes 24580
  370.6 4.3 %collective-permute-start.8 = (bf16[2,2,4,2048]{3,2,1,0:T(4,128)(2,1)S(1)}, bf16[2,2,4,2048]{3,2,1,0:T(4,128)(2,1)S(1)}, u32[]{:S(2)}, u32[]{:S(2)}) collective-permute-start(bf16[2,2,4,2048]{3,2,1,0:T(4,128)(2,1)S(1)} %broadcast_select_fusion.3), channel_id=1, source_target_pairs={{0,16},{16,0},{1,17},{17,1},{2,18},{18,2},{3,19},{19,3},{4,20},{20... | collective-permute-start | bytes 196616 | tf_op jit(solution)/shard_map/ppermute | solution.py:20
  375.4 31.0 %all-to-all-start.5 = ((bf16[16,16,2048]{2,1,0:T(8,128)(2,1)}), bf16[16,16,2048]{2,1,0:T(8,128)(2,1)S(1)}, u32[]{:S(2)}, u32[]{:S(2)}) async-start(bf16[16,16,2048]{2,1,0:T(8,128)(2,1)} %broadcast_select_fusion.2), calls=%async_computation.5 | async-start | bytes 2097152 | tf_op jit(solution)/shard_map/all_to_all | solution.py:28
  383.2 1.3 collective-permute-start.9
  384.5 3.6 collective-permute-start.10
  388.2 9.1 %collective-permute-start.11 = (f32[2,16]{1,0:T(2,128)S(1)}, f32[2,16]{1,0:T(2,128)S(1)}, u32[]{:S(2)}, u32[]{:S(2)}) collective-permute-start(f32[2,16]{1,0:T(2,128)S(1)} %pad_maximum_fusion.3), channel_id=1, source_target_pairs={{0,4},{1,5},{2,6},{3,7},{4,0},{5,1},{6,2},{7,3},{8,12},{9,13},{10,... | collective-permute-start | bytes 392 | tf_op jit(solution)/shard_map/ppermute | solution.py:20
  397.3 8.4 %collective-permute-start.12 = (f32[2,16]{1,0:T(2,128)S(1)}, f32[2,16]{1,0:T(2,128)S(1)}, u32[]{:S(2)}, u32[]{:S(2)}) collective-permute-start(f32[2,16]{1,0:T(2,128)S(1)} %pad_maximum_fusion.4), channel_id=1, source_target_pairs={{0,8},{1,9},{2,10},{3,11},{4,12},{5,13},{6,14},{7,15},{8,0},{9,1},... | collective-permute-start | bytes 392 | tf_op jit(solution)/shard_map/ppermute | solution.py:20
  405.7 3.6 collective-permute-start.13
Sparse Core Ops, SparseCore 0:
  11.4 60.4 all-gather.7
  73.5 31.6 all-gather.9
  106.7 33.1 all-gather.13
  141.3 33.1 all-gather.11
where the time goes:
time: 422 us; the launch traced here: 421 us
  waiting for transfers between devices  264 us (63%)
  starting transfers between devices  49.4 us (12%)
  blocking collectives  30.5 us (7%)
  local copies, waits for them, and re-layouts  21.7 us (5%)
  matrix products  20.9 us (5%)
  other arithmetic  20.1 us (5%)
  between operations  14.3 us (3%)
    ppermute x14, waiting for transfers between devices, exchange(): return lax.ppermute(value, axis, [(i, i ^ bit) for i in range(n)])  93.3 us
    all_gather x1, waiting for transfers between devices, per_device(): lax.all_gather(jnp.concatenate([normed, coded], axis=1), 'ep', axis=0, ti...  58.4 us
    all_gather x1, waiting for transfers between devices, per_device(): up_full = lax.all_gather(up_proj[0], 'grp', axis=0, tiled=True)  34.6 us
    all_gather x1, waiting for transfers between devices, per_device(): gate_full = lax.all_gather(gate_proj[0], 'grp', axis=0, tiled=True)  32.1 us
    all_to_all x1, blocking collectives, relocate(): spread = lax.all_to_all(rows, 'ep', split_axis=0, concat_axis=0, tiled=True)  30.5 us
    all_gather x1, waiting for transfers between devices, per_device(): down_full = lax.all_gather(down_proj[0], 'grp', axis=0, tiled=True)  29.3 us
    ppermute x14, starting transfers between devices, exchange(): return lax.ppermute(value, axis, [(i, i ^ bit) for i in range(n)])  24.7 us
    all_to_all x2, waiting for transfers between devices, relocate(): spread = lax.all_to_all(rows, 'ep', split_axis=0, concat_axis=0, tiled=True)  14.4 us
  transfers between devices with their start and end apart: 23, of which 18 were waited for; matrix products, arithmetic and copies ran while one was open for 8% of the time, Pallas kernels for 0%

commit v1 on v0

--- a/solution.py
+++ b/solution.py
@@ -2,6 +2,22 @@
 import jax.numpy as jnp
 from jax import lax
 from jax.sharding import PartitionSpec as P
+
+
+def collect(x, axis, dim):
+    ways, here, step = (lax.axis_size(axis), lax.axis_index(axis), x.shape[dim])
+    shape = [n * ways if d == dim else n for d, n in enumerate(x.shape)]
+    full = lax.dynamic_update_slice_in_dim(jnp.zeros(shape, x.dtype), x, here * step, axis=dim)
+    going_up = going_down = x
+    for far in range(1, ways // 2 + 1):
+        going_up = lax.ppermute(going_up, axis, [(d, (d + 1) % ways) for d in range(ways)])
+        full = lax.dynamic_update_slice_in_dim(full, going_up, (here - far) % ways * step, axis=dim)
+        if 2 * far < ways:
+            going_down = lax.ppermute(going_down, axis, [(d, (d - 1) % ways) for d in range(ways)])
+            full = lax.dynamic_update_slice_in_dim(
+                full, going_down, (here + far) % ways * step, axis=dim
+            )
+    return full
 
 
 def normalize(rows, gain):
@@ -94,7 +110,7 @@
     parts = split_bf16(slot_gates.reshape(-1, n_slots))
     extra = -(-len(parts) * n_slots // 128) * 128
     coded = jnp.pad(jnp.concatenate(parts, axis=1), ((0, 0), (0, extra - len(parts) * n_slots)))
-    rows = lax.all_gather(jnp.concatenate([normed, coded], axis=1), "ep", axis=0, tiled=True)
+    rows = collect(jnp.concatenate([normed, coded], axis=1), "ep", 0)
     gate_full = lax.all_gather(gate_proj[0], "grp", axis=0, tiled=True)
     up_full = lax.all_gather(up_proj[0], "grp", axis=0, tiled=True)
     down_full = lax.all_gather(down_proj[0], "grp", axis=0, tiled=True)

time: 422 us -> 362 us (0.86)
  waiting for transfers between devices: 264 us -> 154 us
  starting transfers between devices: 49.4 us -> 85 us
  local copies, waits for them, and re-layouts: 21.7 us -> 36 us
    all_gather x1 -> x0, waiting for transfers between devices: 58.4 us -> none  [per_device(): lax.all_gather(jnp.concatenate([normed, coded], axis=1), 'ep', axis=0, ti...]
    ppermute x0 -> x15, starting transfers between devices: none -> 35.9 us  [the longest x7 21.6 us: collect(): lax.ppermute(going_down, axis, [(d, (d - 1) % ways) for d in range(ways)])]
    all_gather x1, waiting for transfers between devices: 32.1 us -> 0.02 us  [per_device(): gate_full = lax.all_gather(gate_proj[0], 'grp', axis=0, tiled=True)]
    ppermute x0 -> x15, waiting for transfers between devices: none -> 30.1 us  [the longest x8 30 us: collect(): lax.ppermute(going_up, axis, [(d, (d + 1) % ways) for d in range(ways)])]
    all_gather x1, waiting for transfers between devices: 29.3 us -> 0.02 us  [per_device(): down_full = lax.all_gather(down_proj[0], 'grp', axis=0, tiled=True)]
    all_gather x1, waiting for transfers between devices: 34.6 us -> 14.7 us  [per_device(): up_full = lax.all_gather(up_proj[0], 'grp', axis=0, tiled=True)]
    dynamic_update_slice x0 -> x15, local copies, waits for them, and re-layouts: none -> 11.5 us  [the longest x8 6.11 us: collect(): lax.dynamic_update_slice_in_dim(full, going_up, (here - far) % ways * ste...]
  transfers between devices with their start and end apart: 23 -> 37, of which waited for: 18 -> 23; matrix products, arithmetic and copies ran while one was open for 8% -> 15% of each run, Pallas kernels for 0% -> 0%
where the time goes in v1:
time: 362 us; the launch traced here: 361 us
  waiting for transfers between devices  154 us (43%)
  starting transfers between devices  85 us (23%)
  local copies, waits for them, and re-layouts  36 us (10%)
  blocking collectives  30.5 us (8%)
  matrix products  20.9 us (6%)
  other arithmetic  20.2 us (6%)
  between operations  14.6 us (4%)
    ppermute x14, waiting for transfers between devices, exchange(): return lax.ppermute(value, axis, [(i, i ^ bit) for i in range(n)])  93.4 us
    all_to_all x1, blocking collectives, relocate(): spread = lax.all_to_all(rows, 'ep', split_axis=0, concat_axis=0, tiled=True)  30.5 us
    ppermute x8, waiting for transfers between devices, collect(): lax.ppermute(going_up, axis, [(d, (d + 1) % ways) for d in range(ways)])  30 us
    ppermute x14, starting transfers between devices, exchange(): return lax.ppermute(value, axis, [(i, i ^ bit) for i in range(n)])  24.5 us
    ppermute x7, starting transfers between devices, collect(): lax.ppermute(going_down, axis, [(d, (d - 1) % ways) for d in range(ways)])  21.6 us
    all_gather x1, waiting for transfers between devices, per_device(): up_full = lax.all_gather(up_proj[0], 'grp', axis=0, tiled=True)  14.7 us
    all_to_all x2, waiting for transfers between devices, relocate(): spread = lax.all_to_all(rows, 'ep', split_axis=0, concat_axis=0, tiled=True)  14.4 us
    ppermute x8, starting transfers between devices, collect(): lax.ppermute(going_up, axis, [(d, (d + 1) % ways) for d in range(ways)])  14.2 us
  transfers between devices with their start and end apart: 37, of which 23 were waited for; matrix products, arithmetic and copies ran while one was open for 15% of the time, Pallas kernels for 0%

profile of v1, /device:TPU:0, one launch (start us, length us, event | category | flops | bytes accessed | tf_op | source)
XLA Modules:
  0.0 361.2 jit_solution(5984902093367620109)
XLA Ops:
  12.0 2.8 broadcast_in_dim.99
  16.0 5.0 %collective-permute-start.1 = (bf16[80,2176]{1,0:T(8,128)(2,1)S(1)}, bf16[80,2176]{1,0:T(8,128)(2,1)S(1)}, u32[]{:S(2)}, u32[]{:S(2)}) collective-permute-start(bf16[80,2176]{1,0:T(8,128)(2,1)S(1)} %get-tuple-element.16), channel_id=1, source_target_pairs={{0,15},{1,0},{2,1},{3,2},{4,3},{5,4},{6,5},{7,6},{8,7},{9,8},{10,9... | collective-permute-start | bytes 1044488 | tf_op jit(solution)/shard_map/ppermute | solution.py:16
  21.4 4.7 %collective-permute-done = bf16[80,2176]{1,0:T(8,128)(2,1)S(1)} collective-permute-done((bf16[80,2176]{1,0:T(8,128)(2,1)S(1)}, bf16[80,2176]{1,0:T(8,128)(2,1)S(1)}, u32[]{:S(2)}, u32[]{:S(2)}) %collective-permute-start) | collective-permute-done | bytes 348192 | tf_op jit(solution)/shard_map/ppermute | solution.py:13
  26.6 3.9 %collective-permute-start.3 = (bf16[80,2176]{1,0:T(8,128)(2,1)S(1)}, bf16[80,2176]{1,0:T(8,128)(2,1)S(1)}, u32[]{:S(2)}, u32[]{:S(2)}) collective-permute-start(bf16[80,2176]{1,0:T(8,128)(2,1)S(1)} %collective-permute-done.1), channel_id=1, source_target_pairs={{0,15},{1,0},{2,1},{3,2},{4,3},{5,4},{6,5},{7,6},{8,7},{9,8},{10,9... | collective-permute-start | bytes 1044488 | tf_op jit(solution)/shard_map/ppermute | solution.py:16
  32.1 3.5 collective-permute-done.2
  37.0 3.0 collective-permute-start.5
  41.6 3.6 collective-permute-done.4
  46.7 2.9 collective-permute-start.7
  51.1 3.5 collective-permute-done.6
  56.4 2.7 collective-permute-start.9
  60.7 3.5 collective-permute-done.8
  66.1 2.5 collective-permute-start.11
  70.1 3.5 collective-permute-done.10
  73.7 2.8 collective-permute-start.12
  79.7 3.5 collective-permute-done.12
  83.2 3.7 %collective-permute-start.14 = (bf16[80,2176]{1,0:T(8,128)(2,1)S(1)}, bf16[80,2176]{1,0:T(8,128)(2,1)S(1)}, u32[]{:S(2)}, u32[]{:S(2)}) collective-permute-start(bf16[80,2176]{1,0:T(8,128)(2,1)S(1)} %collective-permute-done.12), channel_id=1, source_target_pairs={{0,1},{1,2},{2,3},{3,4},{4,5},{5,6},{6,7},{7,8},{8,9},{9,10},{10,1... | collective-permute-start | bytes 1044488 | tf_op jit(solution)/shard_map/ppermute | solution.py:13
  88.4 4.2 %collective-permute-done.14 = bf16[80,2176]{1,0:T(8,128)(2,1)S(1)} collective-permute-done((bf16[80,2176]{1,0:T(8,128)(2,1)S(1)}, bf16[80,2176]{1,0:T(8,128)(2,1)S(1)}, u32[]{:S(2)}, u32[]{:S(2)}) %collective-permute-start.14) | collective-permute-done | bytes 348192 | tf_op jit(solution)/shard_map/ppermute | solution.py:13
  94.6 5.4 %fusion.2 = f32[1280,512]{1,0:T(8,128)S(1)} fusion(bf16[1280,2176]{1,0:T(8,128)(2,1)} %constant_dynamic-update-slice_fusion, bf16[1,2048,512]{2,1,0:T(8,128)(2,1)} %all-gather.7.cloned.1.call-done), kind=kOutput, calls=%fused_computation.9 | convolution fusion | flops 2684354560 | bytes 9961472 | tf_op jit(solution)/shard_map/dot_general | solution.py:122
  100.0 14.7 %all-gather.9.cloned.1.call-done = bf16[1,2048,512]{2,1,0:T(8,128)(2,1)} async-done(((bf16[1,1024,512]{2,1,0:T(8,128)(2,1)}), bf16[1,2048,512]{2,1,0:T(8,128)(2,1)}) %all-gather.9.cloned.1.call-update) | async-done | bytes 2097168 | tf_op jit(solution)/shard_map/all_gather | solution.py:115
  114.8 11.4 %convolution_multiply_fusion = f32[1280,2048]{1,0:T(8,128)} fusion(f32[1280]{0:T(1024)S(1)} %select_reduce_fusion, bf16[1,512,2048]{2,1,0:T(8,128)(2,1)} %all-gather.11.cloned.1.call-done, f32[1280,512]{1,0:T(8,128)S(1)} %fusion.2, bf16[1,2048,512]{2,1,0:T(8,128)(2,1)} %all-gather.9.cloned.1.call-done, bf16[1280,2176]{1,0:T(8,128)(2,1)} %constant_dynamic-update-slice_fusion), kind=kOutput, calls=%fused_computation.4 | convolution fusion | flops 5375262720 | bytes 22549504 | tf_op jit(solution)/shard_map/dot_general | solution.py:125
  126.2 4.5 %fusion.4 = bf16[8,80,2048]{2,1,0:T(8,128)(2,1)} fusion(f32[8,2,80,2048]{3,2,1,0:T(8,128)} %bitcast.151, s32[]{:T(128)S(6)} %select_n.251), kind=kLoop, calls=%fused_computation.11 | loop fusion | bytes 5242884 | tf_op jit(solution)/shard_map/convert_element_type | solution.py:65
  130.7 30.5 %all_to_all.30 = bf16[16,64,512]{2,1,0:T(8,128)(2,1)} all-to-all(bf16[16,64,512]{2,1,0:T(8,128)(2,1)S(1)} %bitcast.153), channel_id=1, replica_groups=mesh['grp'=2,'ep'=16] {'ep'}, dimensions={0} | all-to-all | bytes 2097152 | tf_op jit(solution)/shard_map/all_to_all | solution.py:42
  161.2 5.0 %all-to-all-start.2 = ((bf16[16,64,512]{2,1,0:T(8,128)(2,1)}), bf16[16,64,512]{2,1,0:T(8,128)(2,1)S(1)}, u32[]{:S(2)}, u32[]{:S(2)}) async-start(bf16[16,64,512]{2,1,0:T(8,128)(2,1)} %bitcast.16), calls=%async_computation.2 | async-start | bytes 2097152 | tf_op jit(solution)/shard_map/all_to_all | solution.py:42
  166.2 4.1 %bitcast_add_fusion = f32[8,80,2048]{2,1,0:T(8,128)S(1)} fusion(bf16[8,80,2048]{2,1,0:T(8,128)(2,1)} %collective-permute-done.15, f32[8,2,80,2048]{3,2,1,0:T(8,128)} %bitcast.152, s32[]{:T(128)S(6)} %select_n.250), kind=kLoop, calls=%fused_computation.6 | loop fusion | flops 2621440 | bytes 13107204 | tf_op jit(solution)/shard_map/add | solution.py:65
  170.4 2.3 copy-done
  174.8 14.3 %all-to-all-done.2 = bf16[16,64,512]{2,1,0:T(8,128)(2,1)S(1)} async-done(((bf16[16,64,512]{2,1,0:T(8,128)(2,1)}), bf16[16,64,512]{2,1,0:T(8,128)(2,1)S(1)}, u32[]{:S(2)}, u32[]{:S(2)}) %all-to-all-start.2) | async-done | bytes 1048608 | tf_op jit(solution)/shard_map/all_to_all | solution.py:42
  189.2 7.0 %all-to-all-start.4 = ((bf16[16,16,2048]{2,1,0:T(8,128)(2,1)}), bf16[16,16,2048]{2,1,0:T(8,128)(2,1)}, u32[]{:S(2)}, u32[]{:S(2)}) async-start(bf16[16,16,2048]{2,1,0:T(8,128)(2,1)} %bitcast.18), calls=%async_computation.4 | async-start | bytes 2097152 | tf_op jit(solution)/shard_map/all_to_all | solution.py:42
  197.0 19.4 %collective-permute-done.16 = bf16[4,80,2048]{2,1,0:T(8,128)(2,1)} collective-permute-done((bf16[4,80,2048]{2,1,0:T(8,128)(2,1)S(1)}, bf16[4,80,2048]{2,1,0:T(8,128)(2,1)}, u32[]{:S(2)}, u32[]{:S(2)}) %collective-permute-start.16) | collective-permute-done | bytes 1310752 | tf_op jit(solution)/shard_map/ppermute | solution.py:36
  216.4 2.4 bitcast_add_fusion.1
  219.8 3.7 %collective-permute-start.17 = (bf16[2,80,2048]{2,1,0:T(8,128)(2,1)}, bf16[2,80,2048]{2,1,0:T(8,128)(2,1)}, u32[]{:S(2)}, u32[]{:S(2)}) collective-permute-start(bf16[2,80,2048]{2,1,0:T(8,128)(2,1)} %fusion.22), channel_id=1, source_target_pairs={{0,4},{1,5},{2,6},{3,7},{4,0},{5,1},{6,2},{7,3},{8,12},{9,13},{10,... | collective-permute-start | bytes 1966088 | tf_op jit(solution)/shard_map/ppermute | solution.py:36
  223.5 2.8 gather_fusion.2
  226.3 2.8 gather_fusion.3
  229.1 3.2 broadcast_select_fusion
  232.3 4.9 %all-to-all-start.1 = ((bf16[16,64,512]{2,1,0:T(8,128)(2,1)}), bf16[16,64,512]{2,1,0:T(8,128)(2,1)}, u32[]{:S(2)}, u32[]{:S(2)}) async-start(bf16[16,64,512]{2,1,0:T(8,128)(2,1)} %get-tuple-element.24), calls=%async_computation.1 | async-start | bytes 2097152 | tf_op jit(solution)/shard_map/all_to_all | solution.py:44
  242.6 35.1 %collective-permute-done.18 = bf16[1,80,2048]{2,1,0:T(8,128)(2,1)S(1)} collective-permute-done((bf16[1,80,2048]{2,1,0:T(8,128)(2,1)S(1)}, bf16[1,80,2048]{2,1,0:T(8,128)(2,1)S(1)}, u32[]{:S(2)}, u32[]{:S(2)}) %collective-permute-start.18) | collective-permute-done | bytes 327712 | tf_op jit(solution)/shard_map/ppermute | solution.py:36
  279.0 3.9 %all-to-all-start.3 = ((bf16[16,64,512]{2,1,0:T(8,128)(2,1)}), bf16[16,64,512]{2,1,0:T(8,128)(2,1)S(1)}, u32[]{:S(2)}, u32[]{:S(2)}) async-start(bf16[16,64,512]{2,1,0:T(8,128)(2,1)} %get-tuple-element.23), calls=%async_computation.3 | async-start | bytes 2097152 | tf_op jit(solution)/shard_map/all_to_all | solution.py:44
  286.3 5.7 %collective-permute-done.20 = bf16[2,4,2048]{2,1,0:T(4,128)(2,1)S(1)} collective-permute-done((bf16[2,4,2048]{2,1,0:T(4,128)(2,1)S(1)}, bf16[2,4,2048]{2,1,0:T(4,128)(2,1)S(1)}, u32[]{:S(2)}, u32[]{:S(2)}) %collective-permute-start.20) | collective-permute-done | bytes 32800 | tf_op jit(solution)/shard_map/ppermute | solution.py:36
  292.1 9.4 %collective-permute-done.21 = bf16[2,4,2048]{2,1,0:T(4,128)(2,1)S(1)} collective-permute-done((bf16[2,4,2048]{2,1,0:T(4,128)(2,1)S(1)}, bf16[2,4,2048]{2,1,0:T(4,128)(2,1)S(1)}, u32[]{:S(2)}, u32[]{:S(2)}) %collective-permute-start.21) | collective-permute-done | bytes 32800 | tf_op jit(solution)/shard_map/ppermute | solution.py:36
  301.5 4.6 %collective-permute-start.22 = (bf16[2,4,2048]{2,1,0:T(4,128)(2,1)S(1)}, bf16[2,4,2048]{2,1,0:T(4,128)(2,1)S(1)}, u32[]{:S(2)}, u32[]{:S(2)}) collective-permute-start(bf16[2,4,2048]{2,1,0:T(4,128)(2,1)S(1)} %add.362), channel_id=1, source_target_pairs={{0,8},{1,9},{2,10},{3,11},{4,12},{5,13},{6,14},{7,15},{8,0},{9,1},... | collective-permute-start | bytes 98312 | tf_op jit(solution)/shard_map/ppermute | solution.py:36
  307.9 2.8 collective-permute-done.22
  312.6 2.6 collective-permute-done.23
  315.7 3.7 %all-to-all-start.5 = ((bf16[16,16,2048]{2,1,0:T(8,128)(2,1)}), bf16[16,16,2048]{2,1,0:T(8,128)(2,1)S(1)}, u32[]{:S(2)}, u32[]{:S(2)}) async-start(bf16[16,16,2048]{2,1,0:T(8,128)(2,1)} %broadcast_select_fusion.2), calls=%async_computation.5 | async-start | bytes 2097152 | tf_op jit(solution)/shard_map/all_to_all | solution.py:44
  319.4 3.9 %fusion.45 = (f32[16]{0:T(128)S(1)}, f32[16,1536]{1,0:T(8,128)S(1)}) fusion(bf16[2048,1536]{1,0:T(8,128)(2,1)} %param.25, f32[16,2048]{1,0:T(8,128)S(1)} %reshape.265, f32[2048]{0:T(1024)S(1)} %copy-done.6, f32[16]{0:T(128)S(1)} %rsqrt.21), kind=kOutput, calls=%fused_computation.130 | convolution fusion | flops 100786160 | bytes 6529152 | tf_op jit(solution)/shard_map/dot_general | solution.py:144
  330.4 7.2 %collective-permute-done.26 = f32[2,16]{1,0:T(2,128)S(1)} collective-permute-done((f32[2,16]{1,0:T(2,128)S(1)}, f32[2,16]{1,0:T(2,128)S(1)}, u32[]{:S(2)}, u32[]{:S(2)}) %collective-permute-start.26) | collective-permute-done | bytes 160 | tf_op jit(solution)/shard_map/ppermute | solution.py:36
  337.6 4.4 %collective-permute-start.27 = (f32[2,16]{1,0:T(2,128)S(1)}, f32[2,16]{1,0:T(2,128)S(1)}, u32[]{:S(2)}, u32[]{:S(2)}) collective-permute-start(f32[2,16]{1,0:T(2,128)S(1)} %pad_maximum_fusion.4), channel_id=1, source_target_pairs={{0,8},{1,9},{2,10},{3,11},{4,12},{5,13},{6,14},{7,15},{8,0},{9,1},... | collective-permute-start | bytes 392 | tf_op jit(solution)/shard_map/ppermute | solution.py:36
  342.0 4.0 %collective-permute-done.27 = f32[2,16]{1,0:T(2,128)S(1)} collective-permute-done((f32[2,16]{1,0:T(2,128)S(1)}, f32[2,16]{1,0:T(2,128)S(1)}, u32[]{:S(2)}, u32[]{:S(2)}) %collective-permute-start.27) | collective-permute-done | bytes 160 | tf_op jit(solution)/shard_map/ppermute | solution.py:36
  346.7 3.0 collective-permute-done.28
  350.4 2.3 copy.49
  (132 shorter events, 56.2 us)
Async XLA Ops:
  7.2 87.4 %all-gather.7.cloned.1.call-start = ((), (), s32[]{:S(2)}) async-start(), calls=%async_computation.6 | async-start | bytes 3145728 | tf_op jit(solution)/shard_map/all_gather | solution.py:114
  7.9 92.1 %all-gather.11.cloned.1.call-start = ((), (), s32[]{:S(2)}) async-start(), calls=%async_computation.8 | async-start | bytes 3145728 | tf_op jit(solution)/shard_map/all_gather | solution.py:116
  8.6 106.1 %all-gather.9.cloned.1.call-start = ((), (), s32[]{:S(2)}) async-start(), calls=%async_computation.7 | async-start | bytes 3145728 | tf_op jit(solution)/shard_map/all_gather | solution.py:115
  15.5 10.6 %collective-permute-start = (bf16[80,2176]{1,0:T(8,128)(2,1)S(1)}, bf16[80,2176]{1,0:T(8,128)(2,1)S(1)}, u32[]{:S(2)}, u32[]{:S(2)}) collective-permute-start(bf16[80,2176]{1,0:T(8,128)(2,1)S(1)} %get-tuple-element.16), channel_id=1, source_target_pairs={{0,1},{1,2},{2,3},{3,4},{4,5},{5,6},{6,7},{7,8},{8,9},{9,10},{10,1... | collective-permute-start | bytes 1044488 | tf_op jit(solution)/shard_map/ppermute | solution.py:13
  16.0 10.6 %collective-permute-start.1 = (bf16[80,2176]{1,0:T(8,128)(2,1)S(1)}, bf16[80,2176]{1,0:T(8,128)(2,1)S(1)}, u32[]{:S(2)}, u32[]{:S(2)}) collective-permute-start(bf16[80,2176]{1,0:T(8,128)(2,1)S(1)} %get-tuple-element.16), channel_id=1, source_target_pairs={{0,15},{1,0},{2,1},{3,2},{4,3},{5,4},{6,5},{7,6},{8,7},{9,8},{10,9... | collective-permute-start | bytes 1044488 | tf_op jit(solution)/shard_map/ppermute | solution.py:16
  26.1 9.5 %collective-permute-start.2 = (bf16[80,2176]{1,0:T(8,128)(2,1)S(1)}, bf16[80,2176]{1,0:T(8,128)(2,1)S(1)}, u32[]{:S(2)}, u32[]{:S(2)}) collective-permute-start(bf16[80,2176]{1,0:T(8,128)(2,1)S(1)} %collective-permute-done), channel_id=1, source_target_pairs={{0,1},{1,2},{2,3},{3,4},{4,5},{5,6},{6,7},{7,8},{8,9},{9,10},{10,1... | collective-permute-start | bytes 1044488 | tf_op jit(solution)/shard_map/ppermute | solution.py:13
  26.6 10.4 %collective-permute-start.3 = (bf16[80,2176]{1,0:T(8,128)(2,1)S(1)}, bf16[80,2176]{1,0:T(8,128)(2,1)S(1)}, u32[]{:S(2)}, u32[]{:S(2)}) collective-permute-start(bf16[80,2176]{1,0:T(8,128)(2,1)S(1)} %collective-permute-done.1), channel_id=1, source_target_pairs={{0,15},{1,0},{2,1},{3,2},{4,3},{5,4},{6,5},{7,6},{8,7},{9,8},{10,9... | collective-permute-start | bytes 1044488 | tf_op jit(solution)/shard_map/ppermute | solution.py:16
  35.6 9.5 %collective-permute-start.4 = (bf16[80,2176]{1,0:T(8,128)(2,1)S(1)}, bf16[80,2176]{1,0:T(8,128)(2,1)S(1)}, u32[]{:S(2)}, u32[]{:S(2)}) collective-permute-start(bf16[80,2176]{1,0:T(8,128)(2,1)S(1)} %collective-permute-done.2), channel_id=1, source_target_pairs={{0,1},{1,2},{2,3},{3,4},{4,5},{5,6},{6,7},{7,8},{8,9},{9,10},{10,1... | collective-permute-start | bytes 1044488 | tf_op jit(solution)/shard_map/ppermute | solution.py:13
  37.0 9.7 %collective-permute-start.5 = (bf16[80,2176]{1,0:T(8,128)(2,1)S(1)}, bf16[80,2176]{1,0:T(8,128)(2,1)S(1)}, u32[]{:S(2)}, u32[]{:S(2)}) collective-permute-start(bf16[80,2176]{1,0:T(8,128)(2,1)S(1)} %collective-permute-done.3), channel_id=1, source_target_pairs={{0,15},{1,0},{2,1},{3,2},{4,3},{5,4},{6,5},{7,6},{8,7},{9,8},{10,9... | collective-permute-start | bytes 1044488 | tf_op jit(solution)/shard_map/ppermute | solution.py:16
  45.1 9.5 %collective-permute-start.6 = (bf16[80,2176]{1,0:T(8,128)(2,1)S(1)}, bf16[80,2176]{1,0:T(8,128)(2,1)S(1)}, u32[]{:S(2)}, u32[]{:S(2)}) collective-permute-start(bf16[80,2176]{1,0:T(8,128)(2,1)S(1)} %collective-permute-done.4), channel_id=1, source_target_pairs={{0,1},{1,2},{2,3},{3,4},{4,5},{5,6},{6,7},{7,8},{8,9},{9,10},{10,1... | collective-permute-start | bytes 1044488 | tf_op jit(solution)/shard_map/ppermute | solution.py:13
  46.7 9.7 %collective-permute-start.7 = (bf16[80,2176]{1,0:T(8,128)(2,1)S(1)}, bf16[80,2176]{1,0:T(8,128)(2,1)S(1)}, u32[]{:S(2)}, u32[]{:S(2)}) collective-permute-start(bf16[80,2176]{1,0:T(8,128)(2,1)S(1)} %collective-permute-done.5), channel_id=1, source_target_pairs={{0,15},{1,0},{2,1},{3,2},{4,3},{5,4},{6,5},{7,6},{8,7},{9,8},{10,9... | collective-permute-start | bytes 1044488 | tf_op jit(solution)/shard_map/ppermute | solution.py:16
  54.6 9.5 %collective-permute-start.8 = (bf16[80,2176]{1,0:T(8,128)(2,1)S(1)}, bf16[80,2176]{1,0:T(8,128)(2,1)S(1)}, u32[]{:S(2)}, u32[]{:S(2)}) collective-permute-start(bf16[80,2176]{1,0:T(8,128)(2,1)S(1)} %collective-permute-done.6), channel_id=1, source_target_pairs={{0,1},{1,2},{2,3},{3,4},{4,5},{5,6},{6,7},{7,8},{8,9},{9,10},{10,1... | collective-permute-start | bytes 1044488 | tf_op jit(solution)/shard_map/ppermute | solution.py:13
  56.4 9.7 %collective-permute-start.9 = (bf16[80,2176]{1,0:T(8,128)(2,1)S(1)}, bf16[80,2176]{1,0:T(8,128)(2,1)S(1)}, u32[]{:S(2)}, u32[]{:S(2)}) collective-permute-start(bf16[80,2176]{1,0:T(8,128)(2,1)S(1)} %collective-permute-done.7), channel_id=1, source_target_pairs={{0,15},{1,0},{2,1},{3,2},{4,3},{5,4},{6,5},{7,6},{8,7},{9,8},{10,9... | collective-permute-start | bytes 1044488 | tf_op jit(solution)/shard_map/ppermute | solution.py:16
  64.2 9.5 %collective-permute-start.10 = (bf16[80,2176]{1,0:T(8,128)(2,1)S(1)}, bf16[80,2176]{1,0:T(8,128)(2,1)S(1)}, u32[]{:S(2)}, u32[]{:S(2)}) collective-permute-start(bf16[80,2176]{1,0:T(8,128)(2,1)S(1)} %collective-permute-done.8), channel_id=1, source_target_pairs={{0,1},{1,2},{2,3},{3,4},{4,5},{5,6},{6,7},{7,8},{8,9},{9,10},{10,1... | collective-permute-start | bytes 1044488 | tf_op jit(solution)/shard_map/ppermute | solution.py:13
  66.1 10.4 %collective-permute-start.11 = (bf16[80,2176]{1,0:T(8,128)(2,1)S(1)}, bf16[80,2176]{1,0:T(8,128)(2,1)S(1)}, u32[]{:S(2)}, u32[]{:S(2)}) collective-permute-start(bf16[80,2176]{1,0:T(8,128)(2,1)S(1)} %collective-permute-done.9), channel_id=1, source_target_pairs={{0,15},{1,0},{2,1},{3,2},{4,3},{5,4},{6,5},{7,6},{8,7},{9,8},{10,9... | collective-permute-start | bytes 1044488 | tf_op jit(solution)/shard_map/ppermute | solution.py:16
  73.7 9.5 %collective-permute-start.12 = (bf16[80,2176]{1,0:T(8,128)(2,1)S(1)}, bf16[80,2176]{1,0:T(8,128)(2,1)S(1)}, u32[]{:S(2)}, u32[]{:S(2)}) collective-permute-start(bf16[80,2176]{1,0:T(8,128)(2,1)S(1)} %collective-permute-done.10), channel_id=1, source_target_pairs={{0,1},{1,2},{2,3},{3,4},{4,5},{5,6},{6,7},{7,8},{8,9},{9,10},{10,1... | collective-permute-start | bytes 1044488 | tf_op jit(solution)/shard_map/ppermute | solution.py:13
  76.5 11.2 %collective-permute-start.13 = (bf16[80,2176]{1,0:T(8,128)(2,1)S(1)}, bf16[80,2176]{1,0:T(8,128)(2,1)S(1)}, u32[]{:S(2)}, u32[]{:S(2)}) collective-permute-start(bf16[80,2176]{1,0:T(8,128)(2,1)S(1)} %collective-permute-done.11), channel_id=1, source_target_pairs={{0,15},{1,0},{2,1},{3,2},{4,3},{5,4},{6,5},{7,6},{8,7},{9,8},{10,9... | collective-permute-start | bytes 1044488 | tf_op jit(solution)/shard_map/ppermute | solution.py:16
  83.2 9.4 %collective-permute-start.14 = (bf16[80,2176]{1,0:T(8,128)(2,1)S(1)}, bf16[80,2176]{1,0:T(8,128)(2,1)S(1)}, u32[]{:S(2)}, u32[]{:S(2)}) collective-permute-start(bf16[80,2176]{1,0:T(8,128)(2,1)S(1)} %collective-permute-done.12), channel_id=1, source_target_pairs={{0,1},{1,2},{2,3},{3,4},{4,5},{5,6},{6,7},{7,8},{8,9},{9,10},{10,1... | collective-permute-start | bytes 1044488 | tf_op jit(solution)/shard_map/ppermute | solution.py:13
  126.2 4.5 %copy-start.2 = (bf16[1,1024,512]{2,1,0:T(8,128)(2,1)S(1)}, bf16[1,1024,512]{2,1,0:T(8,128)(2,1)}, u32[]{:S(2)}) copy-start(bf16[1,1024,512]{2,1,0:T(8,128)(2,1)} %param.19) | copy-start | bytes 3145732
  130.7 35.5 %collective-permute-start.15 = (bf16[8,80,2048]{2,1,0:T(8,128)(2,1)}, bf16[8,80,2048]{2,1,0:T(8,128)(2,1)}, u32[]{:S(2)}, u32[]{:S(2)}) collective-permute-start(bf16[8,80,2048]{2,1,0:T(8,128)(2,1)} %fusion.4), channel_id=1, source_target_pairs={{0,1},{1,0},{2,3},{3,2},{4,5},{5,4},{6,7},{7,6},{8,9},{9,8},{10,11... | collective-permute-start | bytes 7864328 | tf_op jit(solution)/shard_map/ppermute | solution.py:36
  161.2 28.0 %all-to-all-start.2 = ((bf16[16,64,512]{2,1,0:T(8,128)(2,1)}), bf16[16,64,512]{2,1,0:T(8,128)(2,1)S(1)}, u32[]{:S(2)}, u32[]{:S(2)}) async-start(bf16[16,64,512]{2,1,0:T(8,128)(2,1)} %bitcast.16), calls=%async_computation.2 | async-start | bytes 2097152 | tf_op jit(solution)/shard_map/all_to_all | solution.py:42
  166.2 30.0 %copy-start.9 = (s32[16]{0:T(128)S(1)}, s32[16]{0:T(128)}, u32[]{:S(2)}) copy-start(s32[16]{0:T(128)} %param.23) | copy-start | bytes 196
  166.2 30.0 %copy-start.8 = (s32[16]{0:T(128)S(1)}, s32[16]{0:T(128)}, u32[]{:S(2)}) copy-start(s32[16]{0:T(128)} %param.22) | copy-start | bytes 196
  170.4 2.3 copy-start
  172.9 43.6 %collective-permute-start.16 = (bf16[4,80,2048]{2,1,0:T(8,128)(2,1)S(1)}, bf16[4,80,2048]{2,1,0:T(8,128)(2,1)}, u32[]{:S(2)}, u32[]{:S(2)}) collective-permute-start(bf16[4,80,2048]{2,1,0:T(8,128)(2,1)S(1)} %fusion.12), channel_id=1, source_target_pairs={{0,2},{1,3},{2,0},{3,1},{4,6},{5,7},{6,4},{7,5},{8,10},{9,11},{10,... | collective-permute-start | bytes 3932168 | tf_op jit(solution)/shard_map/ppermute | solution.py:36
  189.2 7.1 %copy-start.1 = (bf16[16,64,512]{2,1,0:T(8,128)(2,1)}, bf16[16,64,512]{2,1,0:T(8,128)(2,1)S(1)}, u32[]{:S(2)}) copy-start(bf16[16,64,512]{2,1,0:T(8,128)(2,1)S(1)} %all-to-all-done.2) | copy-start | bytes 3145732
  189.2 43.1 %all-to-all-start.4 = ((bf16[16,16,2048]{2,1,0:T(8,128)(2,1)}), bf16[16,16,2048]{2,1,0:T(8,128)(2,1)}, u32[]{:S(2)}, u32[]{:S(2)}) async-start(bf16[16,16,2048]{2,1,0:T(8,128)(2,1)} %bitcast.18), calls=%async_computation.4 | async-start | bytes 2097152 | tf_op jit(solution)/shard_map/all_to_all | solution.py:42
  219.8 18.1 %collective-permute-start.17 = (bf16[2,80,2048]{2,1,0:T(8,128)(2,1)}, bf16[2,80,2048]{2,1,0:T(8,128)(2,1)}, u32[]{:S(2)}, u32[]{:S(2)}) collective-permute-start(bf16[2,80,2048]{2,1,0:T(8,128)(2,1)} %fusion.22), channel_id=1, source_target_pairs={{0,4},{1,5},{2,6},{3,7},{4,0},{5,1},{6,2},{7,3},{8,12},{9,13},{10,... | collective-permute-start | bytes 1966088 | tf_op jit(solution)/shard_map/ppermute | solution.py:36
  229.1 13.3 %copy-start.7 = (s32[2,1,4]{2,1,0:T(1,128)S(1)}, s32[2,1,4]{2,1,0:T(1,128)}, u32[]{:S(2)}) copy-start(s32[2,1,4]{2,1,0:T(1,128)} %param.24) | copy-start | bytes 100
  229.1 49.8 %copy-start.4 = (bf16[2,40,2048]{2,1,0:T(8,128)(2,1)S(1)}, bf16[2,40,2048]{2,1,0:T(8,128)(2,1)}, u32[]{:S(2)}) copy-start(bf16[2,40,2048]{2,1,0:T(8,128)(2,1)} %param.14) | copy-start | bytes 983044
  232.3 46.7 %all-to-all-start.1 = ((bf16[16,64,512]{2,1,0:T(8,128)(2,1)}), bf16[16,64,512]{2,1,0:T(8,128)(2,1)}, u32[]{:S(2)}, u32[]{:S(2)}) async-start(bf16[16,64,512]{2,1,0:T(8,128)(2,1)} %get-tuple-element.24), calls=%async_computation.1 | async-start | bytes 2097152 | tf_op jit(solution)/shard_map/all_to_all | solution.py:44
  239.2 1.1 copy-start.3
  240.3 37.4 %collective-permute-start.18 = (bf16[1,80,2048]{2,1,0:T(8,128)(2,1)S(1)}, bf16[1,80,2048]{2,1,0:T(8,128)(2,1)S(1)}, u32[]{:S(2)}, u32[]{:S(2)}) collective-permute-start(bf16[1,80,2048]{2,1,0:T(8,128)(2,1)S(1)} %dynamic-slice_convert_fusion.2), channel_id=1, source_target_pairs={{0,8},{1,9},{2,10},{3,11},{4,12},{5,13},{6,14},{7,15},{8,0},{9,1},... | collective-permute-start | bytes 983048 | tf_op jit(solution)/shard_map/ppermute | solution.py:36
  278.9 40.5 %copy-start.6 = (f32[2048]{0:T(1024)S(1)}, f32[2048]{0:T(1024)}, u32[]{:S(2)}) copy-start(f32[2048]{0:T(1024)} %param.18) | copy-start | bytes 24580
  279.0 44.3 %copy-start.5 = (bf16[2,40,2048]{2,1,0:T(8,128)(2,1)}, bf16[2,40,2048]{2,1,0:T(8,128)(2,1)S(1)}, u32[]{:S(2)}) copy-start(bf16[2,40,2048]{2,1,0:T(8,128)(2,1)S(1)} %fusion.21) | copy-start | bytes 983044
  279.0 36.6 %all-to-all-start.3 = ((bf16[16,64,512]{2,1,0:T(8,128)(2,1)}), bf16[16,64,512]{2,1,0:T(8,128)(2,1)S(1)}, u32[]{:S(2)}, u32[]{:S(2)}) async-start(bf16[16,64,512]{2,1,0:T(8,128)(2,1)} %get-tuple-element.23), calls=%async_computation.3 | async-start | bytes 2097152 | tf_op jit(solution)/shard_map/all_to_all | solution.py:44
  283.1 1.3 collective-permute-start.19
  284.4 7.6 %collective-permute-start.20 = (bf16[2,4,2048]{2,1,0:T(4,128)(2,1)S(1)}, bf16[2,4,2048]{2,1,0:T(4,128)(2,1)S(1)}, u32[]{:S(2)}, u32[]{:S(2)}) collective-permute-start(bf16[2,4,2048]{2,1,0:T(4,128)(2,1)S(1)} %add.360), channel_id=1, source_target_pairs={{0,2},{1,3},{2,0},{3,1},{4,6},{5,7},{6,4},{7,5},{8,10},{9,11},{10,... | collective-permute-start | bytes 98312 | tf_op jit(solution)/shard_map/ppermute | solution.py:36
  292.0 9.4 %collective-permute-start.21 = (bf16[2,4,2048]{2,1,0:T(4,128)(2,1)S(1)}, bf16[2,4,2048]{2,1,0:T(4,128)(2,1)S(1)}, u32[]{:S(2)}, u32[]{:S(2)}) collective-permute-start(bf16[2,4,2048]{2,1,0:T(4,128)(2,1)S(1)} %add.361), channel_id=1, source_target_pairs={{0,4},{1,5},{2,6},{3,7},{4,0},{5,1},{6,2},{7,3},{8,12},{9,13},{10,... | collective-permute-start | bytes 98312 | tf_op jit(solution)/shard_map/ppermute | solution.py:36
  301.5 9.2 %collective-permute-start.22 = (bf16[2,4,2048]{2,1,0:T(4,128)(2,1)S(1)}, bf16[2,4,2048]{2,1,0:T(4,128)(2,1)S(1)}, u32[]{:S(2)}, u32[]{:S(2)}) collective-permute-start(bf16[2,4,2048]{2,1,0:T(4,128)(2,1)S(1)} %add.362), channel_id=1, source_target_pairs={{0,8},{1,9},{2,10},{3,11},{4,12},{5,13},{6,14},{7,15},{8,0},{9,1},... | collective-permute-start | bytes 98312 | tf_op jit(solution)/shard_map/ppermute | solution.py:36
  310.9 4.3 %collective-permute-start.23 = (bf16[2,2,4,2048]{3,2,1,0:T(4,128)(2,1)S(1)}, bf16[2,2,4,2048]{3,2,1,0:T(4,128)(2,1)S(1)}, u32[]{:S(2)}, u32[]{:S(2)}) collective-permute-start(bf16[2,2,4,2048]{3,2,1,0:T(4,128)(2,1)S(1)} %broadcast_select_fusion.3), channel_id=1, source_target_pairs={{0,16},{16,0},{1,17},{17,1},{2,18},{18,2},{3,19},{19,3},{4,20},{20... | collective-permute-start | bytes 196616 | tf_op jit(solution)/shard_map/ppermute | solution.py:36
  315.7 31.0 %all-to-all-start.5 = ((bf16[16,16,2048]{2,1,0:T(8,128)(2,1)}), bf16[16,16,2048]{2,1,0:T(8,128)(2,1)S(1)}, u32[]{:S(2)}, u32[]{:S(2)}) async-start(bf16[16,16,2048]{2,1,0:T(8,128)(2,1)} %broadcast_select_fusion.2), calls=%async_computation.5 | async-start | bytes 2097152 | tf_op jit(solution)/shard_map/all_to_all | solution.py:44
  323.5 1.3 collective-permute-start.24
  324.8 3.6 %collective-permute-start.25 = (f32[2,16]{1,0:T(2,128)S(1)}, f32[2,16]{1,0:T(2,128)S(1)}, u32[]{:S(2)}, u32[]{:S(2)}) collective-permute-start(f32[2,16]{1,0:T(2,128)S(1)} %pad_maximum_fusion.2), channel_id=1, source_target_pairs={{0,2},{1,3},{2,0},{3,1},{4,6},{5,7},{6,4},{7,5},{8,10},{9,11},{10,... | collective-permute-start | bytes 392 | tf_op jit(solution)/shard_map/ppermute | solution.py:36
  328.5 9.1 %collective-permute-start.26 = (f32[2,16]{1,0:T(2,128)S(1)}, f32[2,16]{1,0:T(2,128)S(1)}, u32[]{:S(2)}, u32[]{:S(2)}) collective-permute-start(f32[2,16]{1,0:T(2,128)S(1)} %pad_maximum_fusion.3), channel_id=1, source_target_pairs={{0,4},{1,5},{2,6},{3,7},{4,0},{5,1},{6,2},{7,3},{8,12},{9,13},{10,... | collective-permute-start | bytes 392 | tf_op jit(solution)/shard_map/ppermute | solution.py:36
  337.6 8.4 %collective-permute-start.27 = (f32[2,16]{1,0:T(2,128)S(1)}, f32[2,16]{1,0:T(2,128)S(1)}, u32[]{:S(2)}, u32[]{:S(2)}) collective-permute-start(f32[2,16]{1,0:T(2,128)S(1)} %pad_maximum_fusion.4), channel_id=1, source_target_pairs={{0,8},{1,9},{2,10},{3,11},{4,12},{5,13},{6,14},{7,15},{8,0},{9,1},... | collective-permute-start | bytes 392 | tf_op jit(solution)/shard_map/ppermute | solution.py:36
  346.0 3.6 %collective-permute-start.28 = (f32[2,16]{1,0:T(2,128)S(1)}, f32[2,16]{1,0:T(2,128)S(1)}, u32[]{:S(2)}, u32[]{:S(2)}) collective-permute-start(f32[2,16]{1,0:T(2,128)S(1)} %pad_maximum_fusion.5), channel_id=1, source_target_pairs={{0,16},{16,0},{1,17},{17,1},{2,18},{18,2},{3,19},{19,3},{4,20},{20... | collective-permute-start | bytes 392 | tf_op jit(solution)/shard_map/ppermute | solution.py:36
Sparse Core Ops, SparseCore 0:
  9.5 35.7 all-gather.6
  46.9 33.1 all-gather.10
  81.6 33.1 all-gather.8
